TPU v7x, 512 devices: a whole 4x8x8 slice. The times are simulated.
512 devices in a mesh: tm: 16 (over x_hi, z), space: 32 (over y, x_lo, core).
Axes of the slice: x: 4 (x_hi: 2, x_lo: 2; x = x_hi * 2 + x_lo), y: 8, z: 8, core: 2. Of those that a mesh axis runs over, the one named last changes fastest.
Arguments:
- start_state: float32 [16, 512, 128, 128], P('tm', 'space'), may hold values from -4 to 4
- solid_fraction: float32 [512, 128, 128], P('space'), may hold values from 0 to 0.3
- coarse_gain: float32 [16, 256, 4096], P('tm', 'space'), may hold values from 0.05 to 1
Outputs:
- fine_end: float32 [16, 512, 128, 128], P('tm', 'space')
- coarse_next: float32 [16, 256, 4096], P('tm', 'space')
All inputs are finite; a program needn't handle non-finite values.
Results may differ from a plain program's by a relative error of at most 0.0003.
Values sent between devices are 32-bit elements; how exact they have to be, the bound alone decides.
A program may use at most 64 MiB of HBM per device.

v0:
```python
import jax
import jax.numpy as jnp
from jax import lax
from jax.sharding import PartitionSpec as P

STEPS = 4


time_step = 0.11
solid_drop = 0.9


def extended_2(cells, sides, width):
    for axis, dim in sides:
        count = lax.axis_size(axis)
        ends = count - 1
        head = lax.slice_in_dim(cells, 0, width, axis=dim)
        tail = lax.slice_in_dim(cells, cells.shape[dim] - width, cells.shape[dim], axis=dim)
        cells = jnp.concatenate(
            [
                lax.ppermute(tail, axis, [(i, (i + 1) % count) for i in range(ends)]),
                cells,
                lax.ppermute(head, axis, [((i + 1) % count, i) for i in range(ends)]),
            ],
            axis=dim,
        )
    return cells


def passed_along(block, axis, distance):
    devices = range(lax.axis_size(axis))
    route = [(i - distance, i) for i in devices if i - distance in devices]
    return lax.ppermute(block, axis, route)


def diffusivity(solute, solid_part):
    square = solute * solute
    return (1.0 - solid_drop * solid_part) * (1.0 + 0.5 * square / (1.0 + square))


def face_fluxes(solute, spread, direction):
    length = solute.shape[direction]
    solute_low = lax.slice_in_dim(solute, 0, length - 1, axis=direction)
    solute_high = lax.slice_in_dim(solute, 1, length, axis=direction)
    spread_low = lax.slice_in_dim(spread, 0, length - 1, axis=direction)
    spread_high = lax.slice_in_dim(spread, 1, length, axis=direction)
    return 0.5 * (spread_low + spread_high) * (solute_high - solute_low)


def side_change(fluxes, direction):
    plane_shape = list(fluxes.shape)
    plane_shape[direction] = 1
    border = jnp.zeros(plane_shape, fluxes.dtype)
    return jnp.concatenate([fluxes, border], direction) - jnp.concatenate(
        [border, fluxes], direction
    )


def inner_step(extended, solid_part, inside):
    spread = diffusivity(extended, solid_part)
    z_fluxes = face_fluxes(extended, spread, 0) * (inside[1:] * inside[:-1])[:, None, None]
    change = z_fluxes[1:] - z_fluxes[:-1]
    middle = extended[1:-1]
    spread_mid = spread[1:-1]
    change = change + side_change(face_fluxes(middle, spread_mid, 1), 1)
    change = change + side_change(face_fluxes(middle, spread_mid, 2), 2)
    return middle + time_step * change


def restrict(volume):
    paired = volume.reshape(volume.shape[0] // 2, 2, volume.shape[1] // 2, 2, volume.shape[2]).sum(
        axis=(1, 3)
    )
    paired = paired[:, :, 0::2] + paired[:, :, 1::2]
    return (0.125 * paired).reshape(paired.shape[0], -1)


def on_device(start_state, solid_fraction, coarse_gain):
    rim_width = 1
    slab_count = lax.axis_size("space")
    slab_index = lax.axis_index("space")
    planes = solid_fraction.shape[0]
    solid_rim = extended_2(solid_fraction, (("space", 0),), rim_width)
    position = slab_index * planes - rim_width + jnp.arange(planes + 2 * rim_width, dtype=jnp.int32)
    inside = ((position >= 0) & (position < slab_count * planes)).astype(jnp.float32)
    solute = start_state[0]
    for _ in range(STEPS // rim_width):
        extended = extended_2(solute, (("space", 0),), rim_width)
        extended = inner_step(extended, solid_rim, inside)
        solute = extended
    coarse_fine = restrict(solute)
    coarse_start = restrict(start_state[0])
    amplify = coarse_gain[0]
    leading = lax.axis_index("tm") == 0
    factor = jnp.where(leading, jnp.float32(0.0), amplify)
    offset = jnp.where(leading, coarse_fine, coarse_fine - amplify * coarse_start)

    def pass_on(number, current):
        incoming = passed_along(current, "tm", 1)
        return factor * incoming + offset

    coarse_next = lax.fori_loop(0, lax.axis_size("tm") - 1, pass_on, offset)
    return (solute[None], coarse_next[None])


def solution(mesh):
    placed = (P("tm", "space", None, None), P("space", None, None), P("tm", "space", None))
    return jax.shard_map(
        on_device,
        mesh=mesh,
        in_specs=placed,
        out_specs=(P("tm", "space", None, None), P("tm", "space", None)),
        check_vma=False,
    )
```

profile of v0, /device:TPU:36, one launch (start us, length us, event | category | flops | bytes accessed | tf_op | source)
XLA Modules:
  0.0 245.6 jit_solution(7388691962109114824)
XLA Ops:
  1.5 2.4 collective-permute-start.4
  6.8 5.8 %collective-permute-start.2 = (f32[1,128,128]{2,1,0:T(8,128)S(1)}, f32[1,128,128]{2,1,0:T(8,128)S(1)}, u32[]{:S(2)}, u32[]{:S(2)}) collective-permute-start(f32[1,128,128]{2,1,0:T(8,128)S(1)} %get-tuple-element.40), channel_id=1, source_target_pairs={{1,0},{2,1},{3,2},{4,3},{5,4},{6,5},{7,6},{8,7},{9,8},{10,9},{11,1... | collective-permute-start | bytes 196616 | tf_op jit(solution)/shard_map/ppermute | solution.py:23
  14.6 5.7 %collective-permute-done.1 = f32[1,128,128]{2,1,0:T(8,128)S(1)} collective-permute-done((f32[1,128,128]{2,1,0:T(8,128)S(1)}, f32[1,128,128]{2,1,0:T(8,128)S(1)}, u32[]{:S(2)}, u32[]{:S(2)}) %collective-permute-start.1) | collective-permute-done | bytes 65568 | tf_op jit(solution)/shard_map/ppermute | solution.py:21
  20.2 2.0 add_multiply_fusion.3
  25.9 2.4 collective-permute-start.5
  28.3 5.3 %collective-permute-done.5 = f32[1,128,128]{2,1,0:T(8,128)S(1)} collective-permute-done((f32[1,128,128]{2,1,0:T(8,128)S(1)}, f32[1,128,128]{2,1,0:T(8,128)S(1)}, u32[]{:S(2)}, u32[]{:S(2)}) %collective-permute-start.5) | collective-permute-done | bytes 65568 | tf_op jit(solution)/shard_map/ppermute | solution.py:21
  38.3 2.4 collective-permute-start.7
  41.4 5.1 %slice.304 = f32[8,64,64]{2,1,0:T(8,128)} slice(f32[8,64,128]{2,1,0:T(8,128)S(1)} %reduce_sum.19), slice={[0:8:1], [0:64:1], [0:128:2]} | slice | bytes 262144 | tf_op jit(solution)/shard_map/slice | solution.py:74
  46.5 5.1 %slice.305 = f32[8,64,64]{2,1,0:T(8,128)} slice(f32[8,64,128]{2,1,0:T(8,128)S(1)} %reduce_sum.19), slice={[0:8:1], [0:64:1], [1:128:2]} | slice | bytes 262144 | tf_op jit(solution)/shard_map/slice | solution.py:74
  55.5 5.3 %collective-permute-start.10 = (f32[1,128,128]{2,1,0:T(8,128)S(1)}, f32[1,128,128]{2,1,0:T(8,128)S(1)}, u32[]{:S(2)}, u32[]{:S(2)}) collective-permute-start(f32[1,128,128]{2,1,0:T(8,128)S(1)} %get-tuple-element.34), channel_id=1, source_target_pairs={{1,0},{2,1},{3,2},{4,3},{5,4},{6,5},{7,6},{8,7},{9,8},{10,9},{11,1... | collective-permute-start | bytes 196616 | tf_op jit(solution)/shard_map/ppermute | solution.py:23
  60.8 2.1 collective-permute-start.9
  63.1 5.4 %collective-permute-done.9 = f32[1,128,128]{2,1,0:T(8,128)S(1)} collective-permute-done((f32[1,128,128]{2,1,0:T(8,128)S(1)}, f32[1,128,128]{2,1,0:T(8,128)S(1)}, u32[]{:S(2)}, u32[]{:S(2)}) %collective-permute-start.9) | collective-permute-done | bytes 65568 | tf_op jit(solution)/shard_map/ppermute | solution.py:21
  71.4 4.5 %slice.302 = f32[8,64,64]{2,1,0:T(8,128)S(1)} slice(f32[8,64,128]{2,1,0:T(8,128)S(1)} %reduce_sum.18), slice={[0:8:1], [0:64:1], [0:128:2]} | slice | bytes 262144 | tf_op jit(solution)/shard_map/slice | solution.py:74
  75.9 4.5 %slice.303 = f32[8,64,64]{2,1,0:T(8,128)S(1)} slice(f32[8,64,128]{2,1,0:T(8,128)S(1)} %reduce_sum.18), slice={[0:8:1], [0:64:1], [1:128:2]} | slice | bytes 262144 | tf_op jit(solution)/shard_map/slice | solution.py:74
  80.6 164.3 %while.10 = (s32[]{:T(128)}, f32[8,4096]{1,0:T(8,128)S(1)}, f32[8,4096]{1,0:T(8,128)S(1)}, f32[8,4096]{1,0:T(8,128)S(1)}, s32[]{:T(128)}) while((s32[]{:T(128)}, f32[8,4096]{1,0:T(8,128)S(1)}, f32[8,4096]{1,0:T(8,128)S(1)}, f32[8,4096]{1,0:T(8,128)S(1)}, s32[]{:T(128)}) %tuple.28), condition=%wide.region_3.4_spmd, body=%wide.region_2.3_spmd.sunk | while | flops 65538 | bytes 1048677 | solution.py:102
  80.6 4.3 %collective-permute-start = (f32[8,4096]{1,0:T(8,128)S(1)}, f32[8,4096]{1,0:T(8,128)S(1)}, u32[]{:S(2)}, u32[]{:S(2)}) collective-permute-start(f32[8,4096]{1,0:T(8,128)S(1)} %get-tuple-element.76), channel_id=1, source_target_pairs={{0,32},{32,64},{64,96},{96,128},{128,160},{160,192},{192,224},{224... | collective-permute-start | bytes 393224 | tf_op jit(solution)/shard_map/while/body/eval_jaxpr/ppermute | solution.py:33
  84.9 9.8 %collective-permute-done = f32[8,4096]{1,0:T(8,128)S(1)} collective-permute-done((f32[8,4096]{1,0:T(8,128)S(1)}, f32[8,4096]{1,0:T(8,128)S(1)}, u32[]{:S(2)}, u32[]{:S(2)}) %collective-permute-start) | collective-permute-done | bytes 131104 | tf_op jit(solution)/shard_map/while/body/eval_jaxpr/ppermute | solution.py:33
  96.7 8.5 %collective-permute-done = f32[8,4096]{1,0:T(8,128)S(1)} collective-permute-done((f32[8,4096]{1,0:T(8,128)S(1)}, f32[8,4096]{1,0:T(8,128)S(1)}, u32[]{:S(2)}, u32[]{:S(2)}) %collective-permute-start) | collective-permute-done | bytes 131104 | tf_op jit(solution)/shard_map/while/body/eval_jaxpr/ppermute | solution.py:33
  107.3 8.5 %collective-permute-done = f32[8,4096]{1,0:T(8,128)S(1)} collective-permute-done((f32[8,4096]{1,0:T(8,128)S(1)}, f32[8,4096]{1,0:T(8,128)S(1)}, u32[]{:S(2)}, u32[]{:S(2)}) %collective-permute-start) | collective-permute-done | bytes 131104 | tf_op jit(solution)/shard_map/while/body/eval_jaxpr/ppermute | solution.py:33
  117.8 9.3 %collective-permute-done = f32[8,4096]{1,0:T(8,128)S(1)} collective-permute-done((f32[8,4096]{1,0:T(8,128)S(1)}, f32[8,4096]{1,0:T(8,128)S(1)}, u32[]{:S(2)}, u32[]{:S(2)}) %collective-permute-start) | collective-permute-done | bytes 131104 | tf_op jit(solution)/shard_map/while/body/eval_jaxpr/ppermute | solution.py:33
  129.0 9.5 %collective-permute-done = f32[8,4096]{1,0:T(8,128)S(1)} collective-permute-done((f32[8,4096]{1,0:T(8,128)S(1)}, f32[8,4096]{1,0:T(8,128)S(1)}, u32[]{:S(2)}, u32[]{:S(2)}) %collective-permute-start) | collective-permute-done | bytes 131104 | tf_op jit(solution)/shard_map/while/body/eval_jaxpr/ppermute | solution.py:33
  140.5 8.7 %collective-permute-done = f32[8,4096]{1,0:T(8,128)S(1)} collective-permute-done((f32[8,4096]{1,0:T(8,128)S(1)}, f32[8,4096]{1,0:T(8,128)S(1)}, u32[]{:S(2)}, u32[]{:S(2)}) %collective-permute-start) | collective-permute-done | bytes 131104 | tf_op jit(solution)/shard_map/while/body/eval_jaxpr/ppermute | solution.py:33
  151.1 8.5 %collective-permute-done = f32[8,4096]{1,0:T(8,128)S(1)} collective-permute-done((f32[8,4096]{1,0:T(8,128)S(1)}, f32[8,4096]{1,0:T(8,128)S(1)}, u32[]{:S(2)}, u32[]{:S(2)}) %collective-permute-start) | collective-permute-done | bytes 131104 | tf_op jit(solution)/shard_map/while/body/eval_jaxpr/ppermute | solution.py:33
  161.6 8.5 %collective-permute-done = f32[8,4096]{1,0:T(8,128)S(1)} collective-permute-done((f32[8,4096]{1,0:T(8,128)S(1)}, f32[8,4096]{1,0:T(8,128)S(1)}, u32[]{:S(2)}, u32[]{:S(2)}) %collective-permute-start) | collective-permute-done | bytes 131104 | tf_op jit(solution)/shard_map/while/body/eval_jaxpr/ppermute | solution.py:33
  172.1 8.5 %collective-permute-done = f32[8,4096]{1,0:T(8,128)S(1)} collective-permute-done((f32[8,4096]{1,0:T(8,128)S(1)}, f32[8,4096]{1,0:T(8,128)S(1)}, u32[]{:S(2)}, u32[]{:S(2)}) %collective-permute-start) | collective-permute-done | bytes 131104 | tf_op jit(solution)/shard_map/while/body/eval_jaxpr/ppermute | solution.py:33
  180.7 1.9 collective-permute-start
  182.6 8.5 %collective-permute-done = f32[8,4096]{1,0:T(8,128)S(1)} collective-permute-done((f32[8,4096]{1,0:T(8,128)S(1)}, f32[8,4096]{1,0:T(8,128)S(1)}, u32[]{:S(2)}, u32[]{:S(2)}) %collective-permute-start) | collective-permute-done | bytes 131104 | tf_op jit(solution)/shard_map/while/body/eval_jaxpr/ppermute | solution.py:33
  193.2 8.5 %collective-permute-done = f32[8,4096]{1,0:T(8,128)S(1)} collective-permute-done((f32[8,4096]{1,0:T(8,128)S(1)}, f32[8,4096]{1,0:T(8,128)S(1)}, u32[]{:S(2)}, u32[]{:S(2)}) %collective-permute-start) | collective-permute-done | bytes 131104 | tf_op jit(solution)/shard_map/while/body/eval_jaxpr/ppermute | solution.py:33
  203.7 8.5 %collective-permute-done = f32[8,4096]{1,0:T(8,128)S(1)} collective-permute-done((f32[8,4096]{1,0:T(8,128)S(1)}, f32[8,4096]{1,0:T(8,128)S(1)}, u32[]{:S(2)}, u32[]{:S(2)}) %collective-permute-start) | collective-permute-done | bytes 131104 | tf_op jit(solution)/shard_map/while/body/eval_jaxpr/ppermute | solution.py:33
  214.2 9.7 %collective-permute-done = f32[8,4096]{1,0:T(8,128)S(1)} collective-permute-done((f32[8,4096]{1,0:T(8,128)S(1)}, f32[8,4096]{1,0:T(8,128)S(1)}, u32[]{:S(2)}, u32[]{:S(2)}) %collective-permute-start) | collective-permute-done | bytes 131104 | tf_op jit(solution)/shard_map/while/body/eval_jaxpr/ppermute | solution.py:33
  225.8 8.5 %collective-permute-done = f32[8,4096]{1,0:T(8,128)S(1)} collective-permute-done((f32[8,4096]{1,0:T(8,128)S(1)}, f32[8,4096]{1,0:T(8,128)S(1)}, u32[]{:S(2)}, u32[]{:S(2)}) %collective-permute-start) | collective-permute-done | bytes 131104 | tf_op jit(solution)/shard_map/while/body/eval_jaxpr/ppermute | solution.py:33
  236.3 8.5 %collective-permute-done = f32[8,4096]{1,0:T(8,128)S(1)} collective-permute-done((f32[8,4096]{1,0:T(8,128)S(1)}, f32[8,4096]{1,0:T(8,128)S(1)}, u32[]{:S(2)}, u32[]{:S(2)}) %collective-permute-start) | collective-permute-done | bytes 131104 | tf_op jit(solution)/shard_map/while/body/eval_jaxpr/ppermute | solution.py:33
  (87 shorter events, 47.6 us)
Async XLA Ops:
  1.5 13.0 %collective-permute-start.4 = (f32[1,128,128]{2,1,0:T(8,128)S(1)}, f32[1,128,128]{2,1,0:T(8,128)S(1)}, u32[]{:S(2)}, u32[]{:S(2)}) collective-permute-start(f32[1,128,128]{2,1,0:T(8,128)S(1)} %get-tuple-element.42), channel_id=1, source_target_pairs={{1,0},{2,1},{3,2},{4,3},{5,4},{6,5},{7,6},{8,7},{9,8},{10,9},{11,1... | collective-permute-start | bytes 196616 | tf_op jit(solution)/shard_map/ppermute | solution.py:23
  4.0 10.6 %collective-permute-start.3 = (f32[1,128,128]{2,1,0:T(8,128)S(1)}, f32[1,128,128]{2,1,0:T(8,128)S(1)}, u32[]{:S(2)}, u32[]{:S(2)}) collective-permute-start(f32[1,128,128]{2,1,0:T(8,128)S(1)} %get-tuple-element.41), channel_id=1, source_target_pairs={{0,1},{1,2},{2,3},{3,4},{4,5},{5,6},{6,7},{7,8},{8,9},{9,10},{10,1... | collective-permute-start | bytes 196616 | tf_op jit(solution)/shard_map/ppermute | solution.py:21
  6.8 7.8 %collective-permute-start.2 = (f32[1,128,128]{2,1,0:T(8,128)S(1)}, f32[1,128,128]{2,1,0:T(8,128)S(1)}, u32[]{:S(2)}, u32[]{:S(2)}) collective-permute-start(f32[1,128,128]{2,1,0:T(8,128)S(1)} %get-tuple-element.40), channel_id=1, source_target_pairs={{1,0},{2,1},{3,2},{4,3},{5,4},{6,5},{7,6},{8,7},{9,8},{10,9},{11,1... | collective-permute-start | bytes 196616 | tf_op jit(solution)/shard_map/ppermute | solution.py:23
  12.5 7.7 %collective-permute-start.1 = (f32[1,128,128]{2,1,0:T(8,128)S(1)}, f32[1,128,128]{2,1,0:T(8,128)S(1)}, u32[]{:S(2)}, u32[]{:S(2)}) collective-permute-start(f32[1,128,128]{2,1,0:T(8,128)S(1)} %get-tuple-element.39), channel_id=1, source_target_pairs={{0,1},{1,2},{2,3},{3,4},{4,5},{5,6},{6,7},{7,8},{8,9},{9,10},{10,1... | collective-permute-start | bytes 196616 | tf_op jit(solution)/shard_map/ppermute | solution.py:21
  20.2 2.0 copy-start
  23.4 10.2 %copy-start.1 = (f32[16,128,128]{2,1,0:T(8,128)S(1)}, f32[16,128,128]{2,1,0:T(8,128)}, u32[]{:S(2)}) copy-start(f32[16,128,128]{2,1,0:T(8,128)} %param.6) | copy-start | bytes 3145732
  24.0 4.3 %collective-permute-start.6 = (f32[1,128,128]{2,1,0:T(8,128)S(1)}, f32[1,128,128]{2,1,0:T(8,128)S(1)}, u32[]{:S(2)}, u32[]{:S(2)}) collective-permute-start(f32[1,128,128]{2,1,0:T(8,128)S(1)} %get-tuple-element.38), channel_id=1, source_target_pairs={{1,0},{2,1},{3,2},{4,3},{5,4},{6,5},{7,6},{8,7},{9,8},{10,9},{11,1... | collective-permute-start | bytes 196616 | tf_op jit(solution)/shard_map/ppermute | solution.py:23
  25.9 7.7 %collective-permute-start.5 = (f32[1,128,128]{2,1,0:T(8,128)S(1)}, f32[1,128,128]{2,1,0:T(8,128)S(1)}, u32[]{:S(2)}, u32[]{:S(2)}) collective-permute-start(f32[1,128,128]{2,1,0:T(8,128)S(1)} %get-tuple-element.37), channel_id=1, source_target_pairs={{0,1},{1,2},{2,3},{3,4},{4,5},{5,6},{6,7},{7,8},{8,9},{9,10},{10,1... | collective-permute-start | bytes 196616 | tf_op jit(solution)/shard_map/ppermute | solution.py:21
  36.3 15.3 %collective-permute-start.8 = (f32[1,128,128]{2,1,0:T(8,128)}, f32[1,128,128]{2,1,0:T(8,128)}, u32[]{:S(2)}, u32[]{:S(2)}) collective-permute-start(f32[1,128,128]{2,1,0:T(8,128)} %get-tuple-element.36), channel_id=1, source_target_pairs={{1,0},{2,1},{3,2},{4,3},{5,4},{6,5},{7,6},{8,7},{9,8},{10,9},{11,1... | collective-permute-start | bytes 196616 | tf_op jit(solution)/shard_map/ppermute | solution.py:23
  38.3 13.4 %collective-permute-start.7 = (f32[1,128,128]{2,1,0:T(8,128)}, f32[1,128,128]{2,1,0:T(8,128)}, u32[]{:S(2)}, u32[]{:S(2)}) collective-permute-start(f32[1,128,128]{2,1,0:T(8,128)} %get-tuple-element.35), channel_id=1, source_target_pairs={{0,1},{1,2},{2,3},{3,4},{4,5},{5,6},{6,7},{7,8},{8,9},{9,10},{10,1... | collective-permute-start | bytes 196616 | tf_op jit(solution)/shard_map/ppermute | solution.py:21
  54.9 8.0 %copy-start.3 = (f32[8,64,64]{2,1,0:T(8,128)S(1)}, f32[8,64,64]{2,1,0:T(8,128)}, u32[]{:S(2)}) copy-start(f32[8,64,64]{2,1,0:T(8,128)} %slice.304) | copy-start | bytes 393220
  54.9 8.0 %copy-start.4 = (f32[8,64,64]{2,1,0:T(8,128)S(1)}, f32[8,64,64]{2,1,0:T(8,128)}, u32[]{:S(2)}) copy-start(f32[8,64,64]{2,1,0:T(8,128)} %slice.305) | copy-start | bytes 393220
  55.5 7.6 %collective-permute-start.10 = (f32[1,128,128]{2,1,0:T(8,128)S(1)}, f32[1,128,128]{2,1,0:T(8,128)S(1)}, u32[]{:S(2)}, u32[]{:S(2)}) collective-permute-start(f32[1,128,128]{2,1,0:T(8,128)S(1)} %get-tuple-element.34), channel_id=1, source_target_pairs={{1,0},{2,1},{3,2},{4,3},{5,4},{6,5},{7,6},{8,7},{9,8},{10,9},{11,1... | collective-permute-start | bytes 196616 | tf_op jit(solution)/shard_map/ppermute | solution.py:23
  60.8 7.7 %collective-permute-start.9 = (f32[1,128,128]{2,1,0:T(8,128)S(1)}, f32[1,128,128]{2,1,0:T(8,128)S(1)}, u32[]{:S(2)}, u32[]{:S(2)}) collective-permute-start(f32[1,128,128]{2,1,0:T(8,128)S(1)} %get-tuple-element.33), channel_id=1, source_target_pairs={{0,1},{1,2},{2,3},{3,4},{4,5},{5,6},{6,7},{7,8},{8,9},{9,10},{10,1... | collective-permute-start | bytes 196616 | tf_op jit(solution)/shard_map/ppermute | solution.py:21
  70.6 9.8 %copy-start.2 = (f32[16,128,128]{2,1,0:T(8,128)}, f32[16,128,128]{2,1,0:T(8,128)S(1)}, u32[]{:S(2)}) copy-start(f32[16,128,128]{2,1,0:T(8,128)S(1)} %fusion.20) | copy-start | bytes 3145732
  71.4 9.2 %copy-start.6 = (f32[1,8,4096]{2,1,0:T(8,128)S(1)}, f32[1,8,4096]{2,1,0:T(8,128)}, u32[]{:S(2)}) copy-start(f32[1,8,4096]{2,1,0:T(8,128)} %param.7) | copy-start | bytes 393220
  80.6 14.1 %collective-permute-start = (f32[8,4096]{1,0:T(8,128)S(1)}, f32[8,4096]{1,0:T(8,128)S(1)}, u32[]{:S(2)}, u32[]{:S(2)}) collective-permute-start(f32[8,4096]{1,0:T(8,128)S(1)} %get-tuple-element.76), channel_id=1, source_target_pairs={{0,32},{32,64},{64,96},{96,128},{128,160},{160,192},{192,224},{224... | collective-permute-start | bytes 393224 | tf_op jit(solution)/shard_map/while/body/eval_jaxpr/ppermute | solution.py:33
  94.8 10.5 %collective-permute-start = (f32[8,4096]{1,0:T(8,128)S(1)}, f32[8,4096]{1,0:T(8,128)S(1)}, u32[]{:S(2)}, u32[]{:S(2)}) collective-permute-start(f32[8,4096]{1,0:T(8,128)S(1)} %get-tuple-element.76), channel_id=1, source_target_pairs={{0,32},{32,64},{64,96},{96,128},{128,160},{160,192},{192,224},{224... | collective-permute-start | bytes 393224 | tf_op jit(solution)/shard_map/while/body/eval_jaxpr/ppermute | solution.py:33
  105.3 10.5 %collective-permute-start = (f32[8,4096]{1,0:T(8,128)S(1)}, f32[8,4096]{1,0:T(8,128)S(1)}, u32[]{:S(2)}, u32[]{:S(2)}) collective-permute-start(f32[8,4096]{1,0:T(8,128)S(1)} %get-tuple-element.76), channel_id=1, source_target_pairs={{0,32},{32,64},{64,96},{96,128},{128,160},{160,192},{192,224},{224... | collective-permute-start | bytes 393224 | tf_op jit(solution)/shard_map/while/body/eval_jaxpr/ppermute | solution.py:33
  115.8 11.2 %collective-permute-start = (f32[8,4096]{1,0:T(8,128)S(1)}, f32[8,4096]{1,0:T(8,128)S(1)}, u32[]{:S(2)}, u32[]{:S(2)}) collective-permute-start(f32[8,4096]{1,0:T(8,128)S(1)} %get-tuple-element.76), channel_id=1, source_target_pairs={{0,32},{32,64},{64,96},{96,128},{128,160},{160,192},{192,224},{224... | collective-permute-start | bytes 393224 | tf_op jit(solution)/shard_map/while/body/eval_jaxpr/ppermute | solution.py:33
  127.1 11.4 %collective-permute-start = (f32[8,4096]{1,0:T(8,128)S(1)}, f32[8,4096]{1,0:T(8,128)S(1)}, u32[]{:S(2)}, u32[]{:S(2)}) collective-permute-start(f32[8,4096]{1,0:T(8,128)S(1)} %get-tuple-element.76), channel_id=1, source_target_pairs={{0,32},{32,64},{64,96},{96,128},{128,160},{160,192},{192,224},{224... | collective-permute-start | bytes 393224 | tf_op jit(solution)/shard_map/while/body/eval_jaxpr/ppermute | solution.py:33
  138.5 10.6 %collective-permute-start = (f32[8,4096]{1,0:T(8,128)S(1)}, f32[8,4096]{1,0:T(8,128)S(1)}, u32[]{:S(2)}, u32[]{:S(2)}) collective-permute-start(f32[8,4096]{1,0:T(8,128)S(1)} %get-tuple-element.76), channel_id=1, source_target_pairs={{0,32},{32,64},{64,96},{96,128},{128,160},{160,192},{192,224},{224... | collective-permute-start | bytes 393224 | tf_op jit(solution)/shard_map/while/body/eval_jaxpr/ppermute | solution.py:33
  149.2 10.5 %collective-permute-start = (f32[8,4096]{1,0:T(8,128)S(1)}, f32[8,4096]{1,0:T(8,128)S(1)}, u32[]{:S(2)}, u32[]{:S(2)}) collective-permute-start(f32[8,4096]{1,0:T(8,128)S(1)} %get-tuple-element.76), channel_id=1, source_target_pairs={{0,32},{32,64},{64,96},{96,128},{128,160},{160,192},{192,224},{224... | collective-permute-start | bytes 393224 | tf_op jit(solution)/shard_map/while/body/eval_jaxpr/ppermute | solution.py:33
  159.7 10.5 %collective-permute-start = (f32[8,4096]{1,0:T(8,128)S(1)}, f32[8,4096]{1,0:T(8,128)S(1)}, u32[]{:S(2)}, u32[]{:S(2)}) collective-permute-start(f32[8,4096]{1,0:T(8,128)S(1)} %get-tuple-element.76), channel_id=1, source_target_pairs={{0,32},{32,64},{64,96},{96,128},{128,160},{160,192},{192,224},{224... | collective-permute-start | bytes 393224 | tf_op jit(solution)/shard_map/while/body/eval_jaxpr/ppermute | solution.py:33
  170.2 10.5 %collective-permute-start = (f32[8,4096]{1,0:T(8,128)S(1)}, f32[8,4096]{1,0:T(8,128)S(1)}, u32[]{:S(2)}, u32[]{:S(2)}) collective-permute-start(f32[8,4096]{1,0:T(8,128)S(1)} %get-tuple-element.76), channel_id=1, source_target_pairs={{0,32},{32,64},{64,96},{96,128},{128,160},{160,192},{192,224},{224... | collective-permute-start | bytes 393224 | tf_op jit(solution)/shard_map/while/body/eval_jaxpr/ppermute | solution.py:33
  180.7 10.5 %collective-permute-start = (f32[8,4096]{1,0:T(8,128)S(1)}, f32[8,4096]{1,0:T(8,128)S(1)}, u32[]{:S(2)}, u32[]{:S(2)}) collective-permute-start(f32[8,4096]{1,0:T(8,128)S(1)} %get-tuple-element.76), channel_id=1, source_target_pairs={{0,32},{32,64},{64,96},{96,128},{128,160},{160,192},{192,224},{224... | collective-permute-start | bytes 393224 | tf_op jit(solution)/shard_map/while/body/eval_jaxpr/ppermute | solution.py:33
  191.2 10.5 %collective-permute-start = (f32[8,4096]{1,0:T(8,128)S(1)}, f32[8,4096]{1,0:T(8,128)S(1)}, u32[]{:S(2)}, u32[]{:S(2)}) collective-permute-start(f32[8,4096]{1,0:T(8,128)S(1)} %get-tuple-element.76), channel_id=1, source_target_pairs={{0,32},{32,64},{64,96},{96,128},{128,160},{160,192},{192,224},{224... | collective-permute-start | bytes 393224 | tf_op jit(solution)/shard_map/while/body/eval_jaxpr/ppermute | solution.py:33
  201.7 10.5 %collective-permute-start = (f32[8,4096]{1,0:T(8,128)S(1)}, f32[8,4096]{1,0:T(8,128)S(1)}, u32[]{:S(2)}, u32[]{:S(2)}) collective-permute-start(f32[8,4096]{1,0:T(8,128)S(1)} %get-tuple-element.76), channel_id=1, source_target_pairs={{0,32},{32,64},{64,96},{96,128},{128,160},{160,192},{192,224},{224... | collective-permute-start | bytes 393224 | tf_op jit(solution)/shard_map/while/body/eval_jaxpr/ppermute | solution.py:33
  212.3 11.6 %collective-permute-start = (f32[8,4096]{1,0:T(8,128)S(1)}, f32[8,4096]{1,0:T(8,128)S(1)}, u32[]{:S(2)}, u32[]{:S(2)}) collective-permute-start(f32[8,4096]{1,0:T(8,128)S(1)} %get-tuple-element.76), channel_id=1, source_target_pairs={{0,32},{32,64},{64,96},{96,128},{128,160},{160,192},{192,224},{224... | collective-permute-start | bytes 393224 | tf_op jit(solution)/shard_map/while/body/eval_jaxpr/ppermute | solution.py:33
  223.9 10.5 %collective-permute-start = (f32[8,4096]{1,0:T(8,128)S(1)}, f32[8,4096]{1,0:T(8,128)S(1)}, u32[]{:S(2)}, u32[]{:S(2)}) collective-permute-start(f32[8,4096]{1,0:T(8,128)S(1)} %get-tuple-element.76), channel_id=1, source_target_pairs={{0,32},{32,64},{64,96},{96,128},{128,160},{160,192},{192,224},{224... | collective-permute-start | bytes 393224 | tf_op jit(solution)/shard_map/while/body/eval_jaxpr/ppermute | solution.py:33
  234.4 10.5 %collective-permute-start = (f32[8,4096]{1,0:T(8,128)S(1)}, f32[8,4096]{1,0:T(8,128)S(1)}, u32[]{:S(2)}, u32[]{:S(2)}) collective-permute-start(f32[8,4096]{1,0:T(8,128)S(1)} %get-tuple-element.76), channel_id=1, source_target_pairs={{0,32},{32,64},{64,96},{96,128},{128,160},{160,192},{192,224},{224... | collective-permute-start | bytes 393224 | tf_op jit(solution)/shard_map/while/body/eval_jaxpr/ppermute | solution.py:33
  244.9 0.7 copy-start.5
where the time goes:
time: 247 us; the launch traced here: 246 us
  waiting for transfers between devices  149 us (60%)
  starting transfers between devices  59.2 us (24%)
  local copies, waits for them, and re-layouts  22.6 us (9%)
  other arithmetic  13.6 us (6%)
    ppermute x15, waiting for transfers between devices, passed_along(): return lax.ppermute(block, axis, route)  132 us
    ppermute x15, starting transfers between devices, passed_along(): return lax.ppermute(block, axis, route)  31.2 us
    slice x4, local copies, waits for them, and re-layouts, restrict(): paired = paired[:, :, 0::2] + paired[:, :, 1::2]  19.3 us
    ppermute x5, starting transfers between devices, extended_2(): lax.ppermute(head, axis, [((i + 1) % count, i) for i in range(ends)])  17.3 us
    ppermute x5, waiting for transfers between devices, extended_2(): lax.ppermute(tail, axis, [(i, (i + 1) % count) for i in range(ends)])  16.3 us
    ppermute x5, starting transfers between devices, extended_2(): lax.ppermute(tail, axis, [(i, (i + 1) % count) for i in range(ends)])  10.8 us
  transfers between devices with their start and end apart: 25, of which 18 were waited for; matrix products, arithmetic and copies ran while one was open for 5% of the time, Pallas kernels for 0%

commit v1 on v0

v1 whole, which is shorter than its diff:
```python
import functools

import jax
import jax.numpy as jnp
from jax import lax
from jax.experimental import pallas as pl
from jax.experimental.pallas import tpu as pltpu
from jax.sharding import PartitionSpec as P

STEPS = 4
H = STEPS
F32 = jnp.float32
MESH = pl.DeviceIdType.MESH

time_step = 0.11
solid_drop = 0.9

ROWS = 32
NP = 2


def kernel(
    nt, ns, c_hbm, s_hbm, g_hbm, fine_ref, coarse_ref,
    c0, c1, c2, c3, c4, d0, d1, d2, d3, bb, fz, fx, vs, ly,
    gv, gl, rs, jl, gb, jb, xb, ob,
    ld_sem, halo_send, halo_recv, g_send, g_recv, j_send, j_recv, x_send, x_recv, out_sem,
):
    planes, nx, ny = c_hbm.shape
    cs = (c0, c1, c2, c3, c4)
    ds = (d0, d1, d2, d3)
    t = lax.axis_index("tm")
    s = lax.axis_index("space")
    core = lax.rem(s, 2)
    step = 2 * core - 1
    first = jnp.where(core == 1, 0, planes + 2 * H - 1)

    def at(q):
        return first + step * q

    barrier = pltpu.get_barrier_semaphore()
    for k in range(1, nt):
        pl.semaphore_signal(barrier, inc=1, device_id={"tm": lax.rem(t + k, nt)}, device_id_type=MESH)
    fast = s + 1 - 2 * core
    slow = s - 1 + 2 * core
    inner = jnp.logical_and(slow >= 0, slow < ns)
    pl.semaphore_signal(barrier, inc=1, device_id={"space": fast}, device_id_type=MESH)

    @pl.when(inner)
    def _():
        pl.semaphore_signal(barrier, inc=1, device_id={"space": slow}, device_id_type=MESH)

    loads = [
        pltpu.make_async_copy(c_hbm, c0.at[pl.ds(H, planes), pl.ds(0, nx)], ld_sem.at[0]),
        pltpu.make_async_copy(s_hbm, bb.at[pl.ds(H, planes)], ld_sem.at[1]),
        pltpu.make_async_copy(g_hbm, gv, ld_sem.at[2]),
    ]
    for cp in loads:
        cp.start()

    row = lax.broadcasted_iota(jnp.int32, (2 * ny, ny), 0)
    lane = lax.broadcasted_iota(jnp.int32, (2 * ny, ny), 1)
    ly[...] = jnp.where(row // 2 == lane, F32(0.125), F32(0.0))
    for l in range(STEPS):
        fx[l, pl.ds(0, 8), :] = jnp.zeros((8, ny), F32)

    def restrict(ref, lo, hi):
        vs[...] = ref[lo, pl.ds(0, nx), :] + ref[hi, pl.ds(0, nx), :]
        parts = []
        for gg in range(2):
            halves = []
            for h in range(2):
                base = 4 * gg + 2 * h
                halves.append(
                    vs[pl.ds(base, nt, stride=8), :] + vs[pl.ds(base + 1, nt, stride=8), :]
                )
            parts.append(jnp.concatenate(halves, axis=1))
        both = jnp.concatenate(parts, axis=0)
        out = jnp.dot(both, ly[...], precision=lax.Precision.HIGHEST, preferred_element_type=F32)
        return out[:nt], out[nt:]

    per = planes // 2 // NP
    rows = 2 * per

    loads[2].wait()
    for g in range(gv.shape[1] // 128):
        v = gv[:, pl.ds(g * 128, 128)]
        for piece in range(NP):
            gl[g // 2, piece, pl.ds(g % 2, per, stride=2), :] = v[piece * per : (piece + 1) * per]

    loads[0].wait()

    @pl.loop(0, planes // 2)
    def _(p):
        piece = p // per
        i = lax.rem(p, per)
        for gg, part in enumerate(restrict(c0, H + 2 * p, H + 2 * p + 1)):
            rs[piece, pl.ds(2 * i + gg, nt, stride=rows), :] = part

    gb[t] = gl[t]
    loads[1].wait()
    pl.semaphore_wait(barrier, jnp.where(inner, nt + 1, nt))

    def sends(to_high, dev, kind, n):
        out = []
        for j in range(H // n):
            src = jnp.where(to_high, planes - n * (j + 1), n * j)
            dst = jnp.where(to_high, H - n * (j + 1), H + planes + n * j)
            for a, (ref, buf) in enumerate(((c_hbm, c0), (s_hbm, bb))):
                to = buf.at[pl.ds(dst, n), pl.ds(0, nx)]
                out.append(
                    pltpu.make_async_remote_copy(
                        src_ref=ref.at[pl.ds(src, n)], dst_ref=to,
                        send_sem=halo_send.at[kind, a, j], recv_sem=halo_recv.at[kind, a, j],
                        device_id={"space": dev}, device_id_type=MESH,
                    )
                )
        return out

    fast_copies = sends(core == 0, fast, 0, H)
    slow_copies = sends(core == 1, slow, 1, 1)
    for cp in fast_copies:
        cp.start()

    @pl.when(inner)
    def _():
        for cp in slow_copies:
            cp.start()

    def mirrors():
        out = []
        for j in range(H):
            src = jnp.where(core == 1, planes - 1 - j, j)
            dst = jnp.where(core == 1, H + planes + j, H - 1 - j)
            for a, (ref, buf) in enumerate(((c_hbm, c0), (s_hbm, bb))):
                out.append(
                    pltpu.make_async_copy(ref.at[src], buf.at[dst, pl.ds(0, nx)], halo_recv.at[1, a, j])
                )
        return out

    @pl.when(jnp.logical_not(inner))
    def _():
        for cp in mirrors():
            cp.start()

    def to_all(src, dst, send, recv):
        for k in range(1, nt):
            q = lax.rem(t + k, nt)
            pltpu.make_async_remote_copy(
                src_ref=src(q), dst_ref=dst, send_sem=send, recv_sem=recv,
                device_id={"tm": q}, device_id_type=MESH,
            ).start()

    def wait_all(ref, sem):
        part = ref.at[pl.ds(0, nt - 1)]
        pltpu.make_async_copy(part, part, sem).wait()

    to_all(lambda q: gl.at[q], gb.at[t], g_send, g_recv)

    def wait_halo(kind, j, n):
        for a, buf in enumerate((c0, bb)):
            part = buf.at[pl.ds(0, n), pl.ds(0, nx)]
            pltpu.make_async_copy(part, part, halo_recv.at[kind, a, j]).wait()

    wait_halo(0, 0, H)

    def spread(c, b):
        return b * (3.0 - 1.0 / (1.0 + c * c))

    def prepare(q):
        p = at(q)
        for r in range(0, nx, ROWS):
            w = pl.ds(r, ROWS)
            b = F32(time_step * 0.25) - F32(time_step * 0.25 * solid_drop) * bb[p, w, :]
            bb[p, w, :] = b
            d0[p, w, :] = spread(c0[p, w, :], b)

    def start_level(l):
        p, b = at(l), at(l - 1)
        c, d = cs[l - 1], ds[l - 1]
        for r in range(0, nx, ROWS):
            w = pl.ds(r, ROWS)
            fz[l - 1, w, :] = (d[b, w, :] + d[p, w, :]) * (c[p, w, :] - c[b, w, :])

    lanes = lax.broadcasted_iota(jnp.int32, (ROWS, ny), 1)
    inside_y = jnp.where(lanes < ny - 1, F32(1.0), F32(0.0))
    rows_in = lax.broadcasted_iota(jnp.int32, (ROWS, ny), 0)
    inside_x = rows_in < ROWS - 1

    def advance(l, q):
        p, a = at(q), at(q + 1)
        c, d = cs[l - 1], ds[l - 1]
        for r in range(0, nx, ROWS):
            w = pl.ds(r, ROWS)
            up = pl.ds(r + 1, ROWS)
            here = c[p, w, :]
            dh = d[p, w, :]
            ahead = (dh + d[a, w, :]) * (c[a, w, :] - here)
            change = ahead - fz[l - 1, w, :]
            fz[l - 1, w, :] = ahead
            flux = (dh + d[p, up, :]) * (c[p, up, :] - here)
            if r + ROWS == nx:
                flux = jnp.where(inside_x, flux, F32(0.0))
            fx[l - 1, pl.ds(r + 8, ROWS), :] = flux
            change = change + (flux - fx[l - 1, pl.ds(r + 7, ROWS), :])
            side = (dh + pltpu.roll(dh, ny - 1, 1)) * (pltpu.roll(here, ny - 1, 1) - here)
            side = side * inside_y
            change = change + (side - pltpu.roll(side, 1, 1))
            new = here + change
            cs[l][p, w, :] = new
            if l < STEPS:
                ds[l][p, w, :] = spread(new, bb[p, w, :])

    def front(k, levels):
        prepare(k + 1)
        for l in range(1, levels + 1):
            advance(l, k - (l - 1))

    prepare(0)
    prepare(1)
    for l in range(1, STEPS):
        start_level(l)
        for k in (2 * l - 1, 2 * l):
            front(k, l)
    start_level(STEPS)

    def body(m):
        @pl.when(m >= planes // 2 - H // 2)
        def _():
            j = 2 * m - (planes - H)
            wait_halo(1, j, 1)
            wait_halo(1, j + 1, 1)

        for k in range(2):
            front(2 * STEPS - 1 + 2 * m + k, STEPS)
        q = H + 2 * m
        lo = jnp.minimum(at(q), at(q + 1))
        pltpu.make_async_copy(
            c4.at[pl.ds(lo, 2)], fine_ref.at[pl.ds(lo - H, 2)], out_sem.at[0]
        ).start()
        plane = (lo - H) // 2
        piece = plane // per
        i = lax.rem(plane, per)
        for gg, part in enumerate(restrict(c4, lo, lo + 1)):
            jl[piece, pl.ds(2 * i + gg, nt, stride=rows), :] = part

    later = jnp.where(t == 0, F32(0.0), F32(1.0))
    order = [jnp.where(core == 1, n, NP - 1 - n) for n in range(NP)]

    for n in range(NP):
        pl.loop(n * per, (n + 1) * per)(body)
        piece = order[n]

        @pl.loop(0, nt)
        def _(o):
            w = pl.ds(pl.multiple_of(o * rows, rows), rows)
            jl[piece, w, :] = jl[piece, w, :] - later * gl[o, piece] * rs[piece, w, :]

        def own(q):
            return pl.ds(pl.multiple_of(q * rows, rows), rows)

        to_all(lambda q: jl.at[piece, own(q)], jb.at[piece, t], j_send.at[n], j_recv.at[n])
        jb[piece, t] = jl[piece, own(t), :]

    wait_all(gb, g_recv)
    for n in range(NP):
        piece = order[n]
        wait_all(jb.at[piece], j_recv.at[n])
        x = jb[piece, 0]
        xb[piece, 0] = x
        for m in range(1, nt):
            x = gb[m, piece] * x + jb[piece, m]
            xb[piece, m] = x
        to_all(lambda q: xb.at[piece, q], ob.at[piece, t], x_send.at[n], x_recv.at[n])
        ob[piece, t] = xb[piece, t]

    for n in range(NP):
        wait_all(ob.at[order[n]], x_recv.at[n])
    for g in range(gv.shape[1] // 128):
        for piece in range(NP):
            coarse_ref[pl.ds(piece * per, per), pl.ds(g * 128, 128)] = ob[
                piece, g // 2, pl.ds(g % 2, per, stride=2), :
            ]

    for cp in fast_copies:
        cp.wait_send()

    @pl.when(inner)
    def _():
        for cp in slow_copies:
            cp.wait_send()

    wait_all(gb, g_send)
    for n in range(NP):
        wait_all(jb.at[0], j_send.at[n])
        wait_all(xb.at[0], x_send.at[n])
    pltpu.make_async_copy(c4.at[pl.ds(0, planes)], fine_ref, out_sem.at[0]).wait()


def on_device(nt, ns, start_state, solid_fraction, coarse_gain):
    planes, nx, ny = solid_fraction.shape
    ext = planes + 2 * H
    cp, cells = coarse_gain.shape[1:]
    rows = cp * cells // 128 // nt // NP
    vmem = lambda *shape: pltpu.VMEM(shape, F32)
    dma = pltpu.SemaphoreType.DMA
    fine, coarse = pl.pallas_call(
        functools.partial(kernel, nt, ns),
        name="parareal",
        out_shape=(
            pltpu.VMEM((planes, nx, ny), F32),
            pltpu.VMEM((cp, cells), F32),
        ),
        in_specs=[pl.BlockSpec(memory_space=pltpu.HBM)] * 3,
        out_specs=(pl.BlockSpec(memory_space=pltpu.VMEM), pl.BlockSpec(memory_space=pltpu.VMEM)),
        scratch_shapes=[
            *[vmem(ext, nx + 8, ny)] * 4, vmem(ext, nx, ny),
            *[vmem(ext, nx + 8, ny)] * 4, vmem(ext, nx, ny),
            vmem(STEPS, nx, ny), vmem(STEPS, nx + 8, ny), vmem(nx, ny), vmem(2 * ny, ny),
            vmem(cp, cells), vmem(nt, NP, rows, 128), vmem(NP, nt * rows, 128), vmem(NP, nt * rows, 128),
            vmem(nt, NP, rows, 128), vmem(NP, nt, rows, 128), vmem(NP, nt, rows, 128), vmem(NP, nt, rows, 128),
            dma((3,)), dma((2, 2, H)), dma((2, 2, H)), dma, dma,
            dma((NP,)), dma((NP,)), dma((NP,)), dma((NP,)), dma((1,)),
        ],
        compiler_params=pltpu.CompilerParams(
            collective_id=0, has_side_effects=True, vmem_limit_bytes=46 * 2**20
        ),
    )(*[pltpu.with_memory_space_constraint(v, pltpu.HBM) for v in (start_state[0], solid_fraction, coarse_gain[0])])
    return fine[None], coarse[None]


def solution(mesh):
    nt, ns = mesh.shape["tm"], mesh.shape["space"]
    placed = (P("tm", "space", None, None), P("space", None, None), P("tm", "space", None))
    return jax.shard_map(
        functools.partial(on_device, nt, ns),
        mesh=mesh,
        in_specs=placed,
        out_specs=(P("tm", "space", None, None), P("tm", "space", None)),
        check_vma=False,
    )
```

time: 247 us -> 44.1 us (0.18)
  the two profiles are of different devices: /device:TPU:36 before, /device:TPU:1 now
where the time goes in v1:
time: 44.1 us; the launch traced here: 44 us
  Pallas kernels  41.7 us (95%)
  local copies, waits for them, and re-layouts  1.63 us (4%)
  between operations  0.64 us (1%)
    pallas_call x1, Pallas kernels, on_device(): pl.pallas_call(functools.partial(kernel, nt, ns), name='parareal', out_sh...  41.7 us
    unnamed x2, local copies, waits for them, and re-layouts  1.63 us

profile of v1, /device:TPU:1, one launch (start us, length us, event | category | flops | bytes accessed | tf_op | source)
XLA Modules:
  0.0 44.0 jit_solution(17461695248717585445)
XLA Ops:
  0.6 41.7 %parareal.1 = (f32[16,128,128]{2,1,0:T(8,128)S(1)}, f32[8,4096]{1,0:T(8,128)S(1)}) custom-call(f32[16,128,128]{2,1,0:T(8,128)} %bitcast.6, f32[16,128,128]{2,1,0:T(8,128)} %s_hbm.1, f32[8,4096]{1,0:T(8,128)} %bitcast.7), custom_call_target="tpu_custom_call" | custom-call | tf_op jit(solution)/shard_map/parareal/pallas_call | solution.py:306
  42.4 1.0 %copy.7 = f32[1,16,128,128]{3,2,1,0:T(8,128)} copy(f32[1,16,128,128]{3,2,1,0:T(8,128)S(1)} %bitcast.4) | data formatting | bytes 2097152
  43.3 0.7 %copy.8 = f32[1,8,4096]{2,1,0:T(8,128)} copy(f32[1,8,4096]{2,1,0:T(8,128)S(1)} %bitcast.5) | data formatting | bytes 262144

commit v2 on v1

v2 whole, which is shorter than its diff:
```python
import functools

import jax
import jax.numpy as jnp
from jax import lax
from jax.experimental import pallas as pl
from jax.experimental.pallas import tpu as pltpu
from jax.sharding import PartitionSpec as P

STEPS = 4
H = STEPS
F32 = jnp.float32
MESH = pl.DeviceIdType.MESH

time_step = 0.11
solid_drop = 0.9

ROWS = 32
NP = 4
EARLY = 4
GROUP = 4


def kernel(
    nt, ns, c_hbm, s_hbm, g_hbm, fine_ref, coarse_ref,
    c0, solid, c1, c2, c3, d0, d1, d2, d3, c_next, d_next, inflow, outflow, fz, vs, ly,
    gv, gl, rs, jl, gb, jb, xb, ob,
    ld_sem, halo_send, halo_recv, g_send, g_recv, j_send, j_recv, x_send, x_recv,
):
    planes, nx, ny = c_hbm.shape
    cs = (c0, c1, c2, c3)
    ds = (d0, d1, d2, d3)
    half = nt // 2
    no = 2 * EARLY
    t = lax.axis_index("tm")
    s = lax.axis_index("space")
    core = lax.rem(s, 2)
    step = 2 * core - 1
    first = jnp.where(core == 1, 0, planes + 2 * H - 1)

    def at(q):
        return first + step * q

    owners = [(o // EARLY) * half + o % EARLY for o in range(no)]
    owner = lax.rem(t, half) < EARLY
    mine = (t // half) * EARLY + lax.rem(t, half)
    group = t // GROUP

    barrier = pltpu.get_barrier_semaphore()

    @pl.when(owner)
    def _():
        for k in range(1, nt):
            pl.semaphore_signal(barrier, inc=1, device_id={"tm": lax.rem(t + k, nt)}, device_id_type=MESH)

    fast = s + 1 - 2 * core
    slow = s - 1 + 2 * core
    inner = jnp.logical_and(slow >= 0, slow < ns)
    pl.semaphore_signal(barrier, inc=1, device_id={"space": fast}, device_id_type=MESH)

    other = lax.rem(t + half, nt)

    @pl.when(inner)
    def _():
        for to in (t, other):
            pl.semaphore_signal(barrier, inc=1, device_id={"tm": to, "space": slow}, device_id_type=MESH)

    loads = [
        pltpu.make_async_copy(c_hbm, c0.at[pl.ds(H, planes)], ld_sem.at[0]),
        pltpu.make_async_copy(s_hbm, solid.at[pl.ds(H, planes)], ld_sem.at[1]),
        pltpu.make_async_copy(g_hbm, gv, ld_sem.at[2]),
    ]
    for cp in loads:
        cp.start()

    def sends(to_high, dev, kind, n, solid_to):
        out = []
        for j in range(H // n):
            src = jnp.where(to_high, planes - n * (j + 1), n * j)
            dst = jnp.where(to_high, H - n * (j + 1), H + planes + n * j)
            for a, (ref, buf) in enumerate(((c_hbm, c0), (s_hbm, solid))):
                to = buf.at[pl.ds(dst, n)]
                out.append(
                    pltpu.make_async_remote_copy(
                        src_ref=ref.at[pl.ds(src, n)], dst_ref=to,
                        send_sem=halo_send.at[kind, a, j], recv_sem=halo_recv.at[kind, a, j],
                        device_id={"tm": (t, solid_to)[a], "space": dev}, device_id_type=MESH,
                    )
                )
        return out

    fast_copies = sends(core == 0, fast, 0, H, t)
    slow_copies = sends(core == 1, slow, 1, 1, other)

    def mirrors():
        out = []
        for j in range(H):
            src = jnp.where(core == 1, planes - 1 - j, j)
            dst = jnp.where(core == 1, H + planes + j, H - 1 - j)
            for a, (ref, buf) in enumerate(((c_hbm, c0), (s_hbm, solid))):
                out.append(
                    pltpu.make_async_copy(ref.at[src], buf.at[dst], halo_recv.at[1, a, j])
                )
        return out

    peers = jnp.where(owner, no, no + 1) + jnp.where(inner, 2, 0)
    pl.semaphore_wait(barrier, peers)

    @pl.when(inner)
    def _():
        for cp in slow_copies:
            cp.start()

    @pl.when(jnp.logical_not(inner))
    def _():
        for cp in mirrors():
            cp.start()

    for cp in fast_copies:
        cp.start()

    row = lax.broadcasted_iota(jnp.int32, (2 * ny, ny), 0)
    lane = lax.broadcasted_iota(jnp.int32, (2 * ny, ny), 1)
    ly[...] = jnp.where(row // 2 == lane, F32(0.125), F32(0.0))

    per = planes // 2 // NP
    groups = 32 // no
    rows = groups * per

    def restrict(ref, lo, hi):
        vs[...] = ref[lo] + ref[hi]
        parts = []
        for gg in range(groups):
            halves = []
            for h in range(2):
                base = 4 * gg + 2 * h
                halves.append(
                    vs[pl.ds(base, no, stride=nx // no), :] + vs[pl.ds(base + 1, no, stride=nx // no), :]
                )
            parts.append(jnp.concatenate(halves, axis=1))
        both = jnp.concatenate(parts, axis=0)
        out = jnp.dot(both, ly[...], precision=lax.Precision.HIGHEST, preferred_element_type=F32)
        return [out[no * gg : no * (gg + 1)] for gg in range(groups)]

    loads[2].wait()
    for g in range(gv.shape[1] // 128):
        v = gv[:, pl.ds(g * 128, 128)]
        for piece in range(NP):
            gl[g // groups, piece, pl.ds(g % groups, per, stride=groups), :] = v[
                piece * per : (piece + 1) * per
            ]

    def to_owners(src, dst, send, recv):
        for o in range(no):
            @pl.when(t != owners[o])
            def _(o=o):
                pltpu.make_async_remote_copy(
                    src_ref=src(o), dst_ref=dst, send_sem=send, recv_sem=recv,
                    device_id={"tm": owners[o]}, device_id_type=MESH,
                ).start()

    def wait_blocks(ref, n, sem):
        part = ref.at[pl.ds(0, n)]
        pltpu.make_async_copy(part, part, sem).wait()

    def wait_either(cond, ref, n, sem):
        @pl.when(cond)
        def _():
            wait_blocks(ref, n - 1, sem)

        @pl.when(jnp.logical_not(cond))
        def _():
            wait_blocks(ref, n, sem)

    to_owners(lambda o: gl.at[o], gb.at[t], g_send, g_recv.at[group])

    @pl.when(owner)
    def _():
        gb[t] = gl[mine]

    loads[0].wait()

    @pl.loop(0, planes // 2)
    def _(p):
        piece = p // per
        i = lax.rem(p, per)
        for gg, part in enumerate(restrict(c0, H + 2 * p, H + 2 * p + 1)):
            rs[piece, pl.ds(groups * i + gg, no, stride=rows), :] = part

    loads[1].wait()

    def wait_halo(kind, j, n):
        for a, buf in enumerate((c0, solid)):
            part = buf.at[pl.ds(0, n)]
            pltpu.make_async_copy(part, part, halo_recv.at[kind, a, j]).wait()

    wait_halo(0, 0, H)

    def spread(c, q, w):
        b = F32(time_step * 0.25) - F32(time_step * 0.25 * solid_drop) * solid[at(q[0] + q[1]), w, :]
        return b * (3.0 - 1.0 / (1.0 + c * c))

    def state(l, q, w):
        return cs[l][q[1] % 2, w, :] if l else c0[at(q[0] + q[1]), w, :]

    def diff(l, q, w):
        return ds[l][q[1] % 2, w, :]

    def after(q, n):
        return (q[0], q[1] + n)

    def store(l, q, w, c):
        i = q[1] % 2
        d = spread(c, q, w)
        if l:
            cs[l][i, w, :] = c
        ds[l][i, w, :] = d
        c_next[l, i, w, :] = pltpu.roll(c, ny - 1, 1)
        d_next[l, i, w, :] = pltpu.roll(d, ny - 1, 1)

    chunks = [pl.ds(r, ROWS) for r in range(0, nx, ROWS)]

    def prepare(q):
        for w in chunks:
            store(0, q, w, c0[at(q[0] + q[1]), w, :])

    def start_level(l):
        q, b = (0, l), (0, l - 1)
        for w in chunks:
            fz[l - 1, w, :] = (diff(l - 1, b, w) + diff(l - 1, q, w)) * (
                state(l - 1, q, w) - state(l - 1, b, w)
            )

    def advance(l, q):
        i = q[1] % 2
        for w in chunks:
            here, dh = state(l - 1, q, w), diff(l - 1, q, w)
            ahead = (dh + diff(l - 1, after(q, 1), w)) * (state(l - 1, after(q, 1), w) - here)
            new = (here + inflow[l - 1, i, w, :]) + (
                (ahead - fz[l - 1, w, :]) - outflow[l - 1, i, w, :]
            )
            fz[l - 1, w, :] = ahead
            if l < STEPS:
                store(l, q, w, new)
            else:
                fine_ref[at(q[0] + q[1]) - H, w, :] = new

    lanes = lax.broadcasted_iota(jnp.int32, (nx, ny), 1)
    rows_in = lax.broadcasted_iota(jnp.int32, (nx, ny), 0)

    def in_plane(l, q):
        i, w = q[1] % 2, pl.ds(0, nx)
        here, dh = state(l, q, w), diff(l, q, w)
        side = (dh + d_next[l, i]) * (c_next[l, i] - here)
        side = jnp.where(lanes < ny - 1, side, F32(0.0))
        outflow[l, i] = pltpu.roll(side, 1, 1)
        flux = (dh + pltpu.roll(dh, nx - 1, 0)) * (pltpu.roll(here, nx - 1, 0) - here)
        flux = jnp.where(rows_in < nx - 1, flux, F32(0.0))
        inflow[l, i] = (flux - pltpu.roll(flux, 1, 0)) + side

    def front(k, levels):
        prepare(after(k, 1))
        for l in range(1, levels + 1):
            advance(l, after(k, 1 - l))
        in_plane(0, after(k, 1))
        for l in range(1, min(levels, STEPS - 1) + 1):
            in_plane(l, after(k, 1 - l))

    prepare((0, 0))
    prepare((0, 1))
    in_plane(0, (0, 1))
    for l in range(1, STEPS):
        start_level(l)
        for k in (2 * l - 1, 2 * l):
            front((0, k), l)
    start_level(STEPS)

    def body(m):
        @pl.when(m >= planes // 2 - H // 2)
        def _():
            j = 2 * m - (planes - H)
            wait_halo(1, j, 1)
            wait_halo(1, j + 1, 1)

        for k in range(2):
            front((2 * m, 2 * STEPS - 1 + k), STEPS)
        q = H + 2 * m
        lo = jnp.minimum(at(q), at(q + 1)) - H
        plane = lo // 2
        piece = plane // per
        i = lax.rem(plane, per)
        for gg, part in enumerate(restrict(fine_ref, lo, lo + 1)):
            jl[piece, pl.ds(groups * i + gg, no, stride=rows), :] = part

    later = jnp.where(t == 0, F32(0.0), F32(1.0))

    def own(o):
        return pl.ds(pl.multiple_of(o * rows, rows), rows)

    @pl.loop(0, NP)
    def _(n):
        pl.loop(n * per, (n + 1) * per)(body)
        piece = jnp.where(core == 1, n, NP - 1 - n)
        for o in range(no):
            w = own(o)
            jl[piece, w, :] = jl[piece, w, :] - later * gl[o, piece] * rs[piece, w, :]
        to_owners(lambda o: jl.at[piece, own(o)], jb.at[piece, t], j_send.at[n], j_recv.at[n, group])

        @pl.when(owner)
        def _():
            jb[piece, t] = jl[piece, own(mine), :]

    def scan(n, gr):
        piece = jnp.where(core == 1, n, NP - 1 - n)
        wait_either(group == gr, jb.at[piece], GROUP, j_recv.at[n, gr])
        for m in range(gr * GROUP, (gr + 1) * GROUP):
            x = jb[piece, m]
            if m:
                x = gb[m, piece] * xb[piece, m - 1] + x
            xb[piece, m] = x
        for m in range(gr * GROUP, (gr + 1) * GROUP):
            @pl.when(t == m)
            def _(m=m):
                ob[piece, mine] = xb[piece, m]

            @pl.when(t != m)
            def _(m=m):
                pltpu.make_async_remote_copy(
                    src_ref=xb.at[piece, m], dst_ref=ob.at[piece, mine],
                    send_sem=x_send.at[n], recv_sem=x_recv.at[n],
                    device_id={"tm": m}, device_id_type=MESH,
                ).start()

    @pl.when(owner)
    def _():
        for grs in ((0,), (1, 2), (3,)):
            for gr in grs:
                wait_either(group == gr, gb, GROUP, g_recv.at[gr])

            @pl.loop(0, NP)
            def _(n):
                for gr in grs:
                    scan(n, gr)

    for n in range(NP):
        wait_either(owner, ob.at[0], no, x_recv.at[n])
    for g in range(gv.shape[1] // 128):
        for piece in range(NP):
            coarse_ref[pl.ds(piece * per, per), pl.ds(g * 128, 128)] = ob[
                piece, g // groups, pl.ds(g % groups, per, stride=groups), :
            ]

    for cp in fast_copies:
        cp.wait_send()

    @pl.when(inner)
    def _():
        for cp in slow_copies:
            cp.wait_send()

    wait_either(owner, gl, no, g_send)
    for n in range(NP):
        wait_either(owner, ob.at[0], no, j_send.at[n])

        @pl.when(owner)
        def _(n=n):
            wait_blocks(xb.at[0], nt - 1, x_send.at[n])


def on_device(nt, ns, start_state, solid_fraction, coarse_gain):
    planes, nx, ny = solid_fraction.shape
    ext = planes + 2 * H
    cp, cells = coarse_gain.shape[1:]
    no = 2 * EARLY
    rows = cp * cells // 128 // no // NP
    vmem = lambda *shape: pltpu.VMEM(shape, F32)
    dma = pltpu.SemaphoreType.DMA
    fine, coarse = pl.pallas_call(
        functools.partial(kernel, nt, ns),
        name="parareal",
        out_shape=(
            pltpu.VMEM((planes, nx, ny), F32),
            pltpu.VMEM((cp, cells), F32),
        ),
        in_specs=[pl.BlockSpec(memory_space=pltpu.HBM)] * 3,
        out_specs=(pl.BlockSpec(memory_space=pltpu.VMEM), pl.BlockSpec(memory_space=pltpu.VMEM)),
        scratch_shapes=[
            *[vmem(ext, nx, ny)] * 2, *[vmem(2, nx, ny)] * 7, *[vmem(STEPS, 2, nx, ny)] * 4,
            vmem(STEPS, nx, ny), vmem(nx, ny), vmem(2 * ny, ny),
            vmem(cp, cells), vmem(no, NP, rows, 128), vmem(NP, no * rows, 128), vmem(NP, no * rows, 128),
            vmem(nt, NP, rows, 128), vmem(NP, nt, rows, 128), vmem(NP, nt, rows, 128), vmem(NP, no, rows, 128),
            dma((3,)), dma((2, 2, H)), dma((2, 2, H)), dma, dma((nt // GROUP,)),
            dma((NP,)), dma((NP, nt // GROUP)), dma((NP,)), dma((NP,)),
        ],
        compiler_params=pltpu.CompilerParams(
            collective_id=0, has_side_effects=True, vmem_limit_bytes=46 * 2**20
        ),
    )(*[pltpu.with_memory_space_constraint(v, pltpu.HBM) for v in (start_state[0], solid_fraction, coarse_gain[0])])
    return fine[None], coarse[None]


def solution(mesh):
    nt, ns = mesh.shape["tm"], mesh.shape["space"]
    placed = (P("tm", "space", None, None), P("space", None, None), P("tm", "space", None))
    return jax.shard_map(
        functools.partial(on_device, nt, ns),
        mesh=mesh,
        in_specs=placed,
        out_specs=(P("tm", "space", None, None), P("tm", "space", None)),
        check_vma=False,
    )
```

time: 44.1 us -> 34.5 us (0.78)
  the two profiles are of different devices: /device:TPU:1 before, /device:TPU:2 now
where the time goes in v2:
time: 34.5 us; the launch traced here: 34.4 us
  Pallas kernels  32.1 us (93%)
  local copies, waits for them, and re-layouts  1.63 us (5%)
  between operations  0.64 us (2%)
    pallas_call x1, Pallas kernels, on_device(): pl.pallas_call(functools.partial(kernel, nt, ns), name='parareal', out_sh...  32.1 us
    unnamed x2, local copies, waits for them, and re-layouts  1.63 us

profile of v2, /device:TPU:2, one launch (start us, length us, event | category | flops | bytes accessed | tf_op | source)
XLA Modules:
  0.0 34.4 jit_solution(14750293016943640615)
XLA Ops:
  0.6 32.1 %parareal.1 = (f32[16,128,128]{2,1,0:T(8,128)S(1)}, f32[8,4096]{1,0:T(8,128)S(1)}) custom-call(f32[16,128,128]{2,1,0:T(8,128)} %bitcast.6, f32[16,128,128]{2,1,0:T(8,128)} %s_hbm.1, f32[8,4096]{1,0:T(8,128)} %bitcast.7), custom_call_target="tpu_custom_call" | custom-call | tf_op jit(solution)/shard_map/parareal/pallas_call | solution.py:378
  32.8 1.0 %copy.7 = f32[1,16,128,128]{3,2,1,0:T(8,128)} copy(f32[1,16,128,128]{3,2,1,0:T(8,128)S(1)} %bitcast.4) | data formatting | bytes 2097152
  33.7 0.7 %copy.8 = f32[1,8,4096]{2,1,0:T(8,128)} copy(f32[1,8,4096]{2,1,0:T(8,128)S(1)} %bitcast.5) | data formatting | bytes 262144

commit v3 on v2

--- a/solution.py
+++ b/solution.py
@@ -17,7 +17,6 @@
 
 ROWS = 32
 NP = 4
-EARLY = 4
 GROUP = 4
 
 
@@ -25,13 +24,13 @@
     nt, ns, c_hbm, s_hbm, g_hbm, fine_ref, coarse_ref,
     c0, solid, c1, c2, c3, d0, d1, d2, d3, c_next, d_next, inflow, outflow, fz, vs, ly,
     gv, gl, rs, jl, gb, jb, xb, ob,
-    ld_sem, halo_send, halo_recv, g_send, g_recv, j_send, j_recv, x_send, x_recv,
+    ld_sem, halo_send, halo_recv, g_send, g_recv, j_send, j_recv, x_send, x_recv, ready,
 ):
     planes, nx, ny = c_hbm.shape
     cs = (c0, c1, c2, c3)
     ds = (d0, d1, d2, d3)
     half = nt // 2
-    no = 2 * EARLY
+    no = nt
     t = lax.axis_index("tm")
     s = lax.axis_index("space")
     core = lax.rem(s, 2)
@@ -41,17 +40,15 @@
     def at(q):
         return first + step * q
 
-    owners = [(o // EARLY) * half + o % EARLY for o in range(no)]
-    owner = lax.rem(t, half) < EARLY
-    mine = (t // half) * EARLY + lax.rem(t, half)
+    place = lax.rem(t, half)
     group = t // GROUP
+    partners = [lax.rem(t + k, nt) for k in range(1, nt)]
 
     barrier = pltpu.get_barrier_semaphore()
-
-    @pl.when(owner)
-    def _():
-        for k in range(1, nt):
-            pl.semaphore_signal(barrier, inc=1, device_id={"tm": lax.rem(t + k, nt)}, device_id_type=MESH)
+    for q in partners:
+        @pl.when(lax.rem(q, half) >= place)
+        def _(q=q):
+            pl.semaphore_signal(barrier, inc=1, device_id={"tm": q}, device_id_type=MESH)
 
     fast = s + 1 - 2 * core
     slow = s - 1 + 2 * core
@@ -103,8 +100,7 @@
                 )
         return out
 
-    peers = jnp.where(owner, no, no + 1) + jnp.where(inner, 2, 0)
-    pl.semaphore_wait(barrier, peers)
+    pl.semaphore_wait(barrier, 2 * place + 2 + jnp.where(inner, 2, 0))
 
     @pl.when(inner)
     def _():
@@ -118,6 +114,11 @@
 
     for cp in fast_copies:
         cp.start()
+
+    for q in partners:
+        @pl.when(lax.rem(q, half) < place)
+        def _(q=q):
+            pl.semaphore_signal(ready, inc=1, device_id={"tm": q}, device_id_type=MESH)
 
     row = lax.broadcasted_iota(jnp.int32, (2 * ny, ny), 0)
     lane = lax.broadcasted_iota(jnp.int32, (2 * ny, ny), 1)
@@ -151,13 +152,11 @@
             ]
 
     def to_owners(src, dst, send, recv):
-        for o in range(no):
-            @pl.when(t != owners[o])
-            def _(o=o):
-                pltpu.make_async_remote_copy(
-                    src_ref=src(o), dst_ref=dst, send_sem=send, recv_sem=recv,
-                    device_id={"tm": owners[o]}, device_id_type=MESH,
-                ).start()
+        for q in partners:
+            pltpu.make_async_remote_copy(
+                src_ref=src(q), dst_ref=dst, send_sem=send, recv_sem=recv,
+                device_id={"tm": q}, device_id_type=MESH,
+            ).start()
 
     def wait_blocks(ref, n, sem):
         part = ref.at[pl.ds(0, n)]
@@ -172,11 +171,7 @@
         def _():
             wait_blocks(ref, n, sem)
 
-    to_owners(lambda o: gl.at[o], gb.at[t], g_send, g_recv.at[group])
-
-    @pl.when(owner)
-    def _():
-        gb[t] = gl[mine]
+    gb[t] = gl[t]
 
     loads[0].wait()
 
@@ -304,11 +299,17 @@
         for o in range(no):
             w = own(o)
             jl[piece, w, :] = jl[piece, w, :] - later * gl[o, piece] * rs[piece, w, :]
+
+        @pl.when(n == 0)
+        def _():
+            @pl.when(place < half - 1)
+            def _():
+                pl.semaphore_wait(ready, 2 * (half - 1 - place))
+
+            to_owners(lambda o: gl.at[o], gb.at[t], g_send, g_recv.at[group])
+
         to_owners(lambda o: jl.at[piece, own(o)], jb.at[piece, t], j_send.at[n], j_recv.at[n, group])
-
-        @pl.when(owner)
-        def _():
-            jb[piece, t] = jl[piece, own(mine), :]
+        jb[piece, t] = jl[piece, own(t), :]
 
     def scan(n, gr):
         piece = jnp.where(core == 1, n, NP - 1 - n)
@@ -321,29 +322,27 @@
         for m in range(gr * GROUP, (gr + 1) * GROUP):
             @pl.when(t == m)
             def _(m=m):
-                ob[piece, mine] = xb[piece, m]
+                ob[piece, t] = xb[piece, m]
 
             @pl.when(t != m)
             def _(m=m):
                 pltpu.make_async_remote_copy(
-                    src_ref=xb.at[piece, m], dst_ref=ob.at[piece, mine],
+                    src_ref=xb.at[piece, m], dst_ref=ob.at[piece, t],
                     send_sem=x_send.at[n], recv_sem=x_recv.at[n],
                     device_id={"tm": m}, device_id_type=MESH,
                 ).start()
 
-    @pl.when(owner)
-    def _():
-        for grs in ((0,), (1, 2), (3,)):
+    for grs in ((0,), (1, 2), (3,)):
+        for gr in grs:
+            wait_either(group == gr, gb, GROUP, g_recv.at[gr])
+
+        @pl.loop(0, NP)
+        def _(n):
             for gr in grs:
-                wait_either(group == gr, gb, GROUP, g_recv.at[gr])
-
-            @pl.loop(0, NP)
-            def _(n):
-                for gr in grs:
-                    scan(n, gr)
+                scan(n, gr)
 
     for n in range(NP):
-        wait_either(owner, ob.at[0], no, x_recv.at[n])
+        wait_blocks(ob.at[0], no - 1, x_recv.at[n])
     for g in range(gv.shape[1] // 128):
         for piece in range(NP):
             coarse_ref[pl.ds(piece * per, per), pl.ds(g * 128, 128)] = ob[
@@ -358,20 +357,17 @@
         for cp in slow_copies:
             cp.wait_send()
 
-    wait_either(owner, gl, no, g_send)
+    wait_blocks(gl, no - 1, g_send)
     for n in range(NP):
-        wait_either(owner, ob.at[0], no, j_send.at[n])
-
-        @pl.when(owner)
-        def _(n=n):
-            wait_blocks(xb.at[0], nt - 1, x_send.at[n])
+        wait_blocks(ob.at[0], no - 1, j_send.at[n])
+        wait_blocks(xb.at[0], nt - 1, x_send.at[n])
 
 
 def on_device(nt, ns, start_state, solid_fraction, coarse_gain):
     planes, nx, ny = solid_fraction.shape
     ext = planes + 2 * H
     cp, cells = coarse_gain.shape[1:]
-    no = 2 * EARLY
+    no = nt
     rows = cp * cells // 128 // no // NP
     vmem = lambda *shape: pltpu.VMEM(shape, F32)
     dma = pltpu.SemaphoreType.DMA
@@ -390,7 +386,7 @@
             vmem(cp, cells), vmem(no, NP, rows, 128), vmem(NP, no * rows, 128), vmem(NP, no * rows, 128),
             vmem(nt, NP, rows, 128), vmem(NP, nt, rows, 128), vmem(NP, nt, rows, 128), vmem(NP, no, rows, 128),
             dma((3,)), dma((2, 2, H)), dma((2, 2, H)), dma, dma((nt // GROUP,)),
-            dma((NP,)), dma((NP, nt // GROUP)), dma((NP,)), dma((NP,)),
+            dma((NP,)), dma((NP, nt // GROUP)), dma((NP,)), dma((NP,)), pltpu.SemaphoreType.REGULAR,
         ],
         compiler_params=pltpu.CompilerParams(
             collective_id=0, has_side_effects=True, vmem_limit_bytes=46 * 2**20

time: 34.5 us -> 33.4 us (0.968)
  the two profiles are of different devices: /device:TPU:2 before, /device:TPU:36 now
where the time goes in v3:
time: 33.4 us; the launch traced here: 33.2 us
  Pallas kernels  30.9 us (93%)
  local copies, waits for them, and re-layouts  1.63 us (5%)
  between operations  0.64 us (2%)
    pallas_call x1, Pallas kernels, on_device(): pl.pallas_call(functools.partial(kernel, nt, ns), name='parareal', out_sh...  30.9 us
    unnamed x2, local copies, waits for them, and re-layouts  1.63 us

profile of v3, /device:TPU:36, one launch (start us, length us, event | category | flops | bytes accessed | tf_op | source)
XLA Modules:
  0.0 33.2 jit_solution(12750142291396352853)
XLA Ops:
  0.6 30.9 %parareal.1 = (f32[16,128,128]{2,1,0:T(8,128)S(1)}, f32[8,4096]{1,0:T(8,128)S(1)}) custom-call(f32[16,128,128]{2,1,0:T(8,128)} %bitcast.6, f32[16,128,128]{2,1,0:T(8,128)} %s_hbm.1, f32[8,4096]{1,0:T(8,128)} %bitcast.7), custom_call_target="tpu_custom_call" | custom-call | tf_op jit(solution)/shard_map/parareal/pallas_call | solution.py:374
  31.6 1.0 %copy.7 = f32[1,16,128,128]{3,2,1,0:T(8,128)} copy(f32[1,16,128,128]{3,2,1,0:T(8,128)S(1)} %bitcast.4) | data formatting | bytes 2097152
  32.5 0.7 %copy.8 = f32[1,8,4096]{2,1,0:T(8,128)} copy(f32[1,8,4096]{2,1,0:T(8,128)S(1)} %bitcast.5) | data formatting | bytes 262144

commit v4 on v3

--- a/solution.py
+++ b/solution.py
@@ -315,9 +315,12 @@
         piece = jnp.where(core == 1, n, NP - 1 - n)
         wait_either(group == gr, jb.at[piece], GROUP, j_recv.at[n, gr])
         for m in range(gr * GROUP, (gr + 1) * GROUP):
-            x = jb[piece, m]
-            if m:
-                x = gb[m, piece] * xb[piece, m - 1] + x
+            if m == 0:
+                x = jb[piece, m]
+            elif m == gr * GROUP:
+                x = gb[m, piece] * xb[piece, m - 1] + jb[piece, m]
+            else:
+                x = gb[m, piece] * x + jb[piece, m]
             xb[piece, m] = x
         for m in range(gr * GROUP, (gr + 1) * GROUP):
             @pl.when(t == m)
@@ -343,11 +346,13 @@
 
     for n in range(NP):
         wait_blocks(ob.at[0], no - 1, x_recv.at[n])
-    for g in range(gv.shape[1] // 128):
-        for piece in range(NP):
-            coarse_ref[pl.ds(piece * per, per), pl.ds(g * 128, 128)] = ob[
-                piece, g // groups, pl.ds(g % groups, per, stride=groups), :
-            ]
+        for at_piece, here in ((n, core == 1), (NP - 1 - n, core == 0)):
+            @pl.when(here)
+            def _(piece=at_piece):
+                for g in range(gv.shape[1] // 128):
+                    coarse_ref[pl.ds(piece * per, per), pl.ds(g * 128, 128)] = ob[
+                        piece, g // groups, pl.ds(g % groups, per, stride=groups), :
+                    ]
 
     for cp in fast_copies:
         cp.wait_send()

time: 33.4 us -> 33.3 us (level)
  no operation moved by 1% of the time
where the time goes in v4:
time: 33.3 us; the launch traced here: 33.1 us
  Pallas kernels  30.9 us (93%)
  local copies, waits for them, and re-layouts  1.63 us (5%)
  between operations  0.64 us (2%)
    pallas_call x1, Pallas kernels, on_device(): pl.pallas_call(functools.partial(kernel, nt, ns), name='parareal', out_sh...  30.9 us
    unnamed x2, local copies, waits for them, and re-layouts  1.63 us

profile of v4, /device:TPU:36, one launch (start us, length us, event | category | flops | bytes accessed | tf_op | source)
XLA Modules:
  0.0 33.1 jit_solution(4500091555080970945)
XLA Ops:
  0.6 30.9 %parareal.1 = (f32[16,128,128]{2,1,0:T(8,128)S(1)}, f32[8,4096]{1,0:T(8,128)S(1)}) custom-call(f32[16,128,128]{2,1,0:T(8,128)} %bitcast.6, f32[16,128,128]{2,1,0:T(8,128)} %s_hbm.1, f32[8,4096]{1,0:T(8,128)} %bitcast.7), custom_call_target="tpu_custom_call" | custom-call | tf_op jit(solution)/shard_map/parareal/pallas_call | solution.py:379
  31.5 1.0 %copy.7 = f32[1,16,128,128]{3,2,1,0:T(8,128)} copy(f32[1,16,128,128]{3,2,1,0:T(8,128)S(1)} %bitcast.4) | data formatting | bytes 2097152
  32.5 0.7 %copy.8 = f32[1,8,4096]{2,1,0:T(8,128)} copy(f32[1,8,4096]{2,1,0:T(8,128)S(1)} %bitcast.5) | data formatting | bytes 262144
